TPU v7x, 256 devices: a whole 4x4x8 slice. The times are simulated.
256 devices in a mesh: gx: 32 (over x, z), gy: 8 (over y, core).
Axes of the slice: x: 4, y: 4, z: 8, core: 2. Of those that a mesh axis runs over, the one named last changes fastest.
Arguments:
- velocity: float32 [3, 16, 4096, 1024], P(None, None, 'gx', 'gy'), may hold values from -6 to 6
- inv_x: float32 [4096, 128], P('gx'), as said below
- inv_y: float32 [1024, 128], P('gy'), as said below
- spike_x: float32 [4096, 2], P('gx'), as said below
- spike_y: float32 [1024, 2], P('gy'), as said below
- marker_force: bfloat16 [3, 524288], P(None, ('gx', 'gy')), may hold values from -6 to 6
- marker_kernel: bfloat16 [524288, 128], P(('gx', 'gy')), may hold values from 0 to 1
- marker_owner: int32 [524288, 1], P(('gx', 'gy')), may hold values from 0 to 31; in each aligned block of 2048 rows (0 to 2047, 2048 to 4095, ...) at most 128 rows name the same one
- marker_row: int32 [524288], P(('gx', 'gy')), may hold values from 0 to 2047
Outputs:
- section_velocity: float32 [3, 16, 4096, 1024], P(None, None, 'gx', 'gy')
Inputs may be any that keep to these rules, and one draw needn't show every extreme that they name: `marker_owner`: among the 2048 marker slots of one device, no owner is named more than 128 times, a bound that some block reaches; every owner is named somewhere. `inv_x`: one block for each streamwise block of cells. `inv_y`: one block for each spanwise block of cells. `spike_x`: two columns for each streamwise block of cells. `spike_y`: two columns for each spanwise block of cells.
All inputs are finite; a program needn't handle non-finite values.
Results may differ from a plain program's by a relative error of at most 0.00046.
Values may be sent and summed in bfloat16 or wider, within the bound.
A program may use at most 128 MiB of HBM per device.

v0:
```python
import functools

import jax
import jax.numpy as jnp
from jax import lax
from jax.experimental import pallas as pl
from jax.experimental.pallas import tpu as pltpu
from jax.sharding import PartitionSpec as P

HIGH = lax.Precision.HIGHEST
MESH = pl.DeviceIdType.MESH
F32, BF16 = jnp.float32, jnp.bfloat16
N = 128
CAP = 128
BLOCK = CAP + 16
NEAR, FAR = 7.0 / 9.0, 1.0 / 36.0


def iota(shape, dim):
    return lax.broadcasted_iota(jnp.int32, shape, dim)


def mm(a, b):
    return jnp.dot(a, b, preferred_element_type=F32)


def mm_nt(a, b, precision=None):
    return lax.dot_general(a, b, (((1,), (1,)), ((), ())), precision=precision, preferred_element_type=F32)


def split(a):
    hi = a.astype(BF16)
    return hi, (a - hi.astype(F32)).astype(BF16)


def inner_stencil(cell, row):
    gap = cell - row
    return jnp.where(gap == 1, NEAR, 0.0) - jnp.where(gap == -1, NEAR, 0.0) + jnp.where(gap == 2, FAR, 0.0) - jnp.where(gap == -2, FAR, 0.0)


def outer_stencil(row, column, first):
    which = column - first
    low2 = jnp.where((which == 0) & (row == 0), -FAR, 0.0)
    low1 = jnp.where((which == 1) & (row == 0), -NEAR, 0.0) + jnp.where((which == 1) & (row == 1), -FAR, 0.0)
    high1 = jnp.where((which == 2) & (row == N - 1), NEAR, 0.0) + jnp.where((which == 2) & (row == N - 2), FAR, 0.0)
    high2 = jnp.where((which == 3) & (row == N - 1), FAR, 0.0)
    return low2 + low1 + high1 + high2


def last_rows(inverse, spike_t):
    sub, lane = iota((N, N), 0), iota((N, N), 1)
    inner_t = inner_stencil(sub, lane)
    spread = [
        mm_nt(inner_t, jnp.broadcast_to(inverse[N - 2 + a : N - 1 + a, :], (N, N)), HIGH) for a in range(2)
    ]
    outer = jnp.dot(inverse[N - 8 :, :], outer_stencil(sub, lane, 0), precision=HIGH, preferred_element_type=F32)
    part, column = iota((2, N), 0), iota((2, N), 1)
    place = iota((1, N), 1)
    rows = []
    for a in range(2):
        row = outer[6 + a : 7 + a, :]
        for b in range(2):
            picked = jnp.where((part == b) & (column == N - 2 + a), spike_t, 0.0)
            value = jnp.sum(jnp.sum(picked, axis=1, keepdims=True), axis=0, keepdims=True)
            row = row + jnp.where(place == 4 + b, value, 0.0)
        rows.append(row)
    return spread, rows


def chain_y(count, got, reply):
    zero = jnp.zeros(got.shape[1:3] + (1, N), F32)

    def one(d, carry):
        s0, s1, low2, low1 = carry
        here = got[d]
        after = got[jnp.minimum(d + 1, count - 1)]
        more = (d + 1 < count).astype(F32)
        high1, high2 = after[:, :, 2:3, :] * more, after[:, :, 3:4, :] * more
        reply[d] = jnp.concatenate([s0, s1, low2, low1, high1, high2, zero, zero], axis=2)
        new = []
        for a in range(2):
            weight = here[:, :, 6 + a : 7 + a, :]
            total = here[:, :, a : a + 1, :]
            for k, value in enumerate((low2, low1, high1, high2, s0, s1)):
                total = total + weight[:, :, :, k : k + 1] * value
            new.append(total)
        return new[0], new[1], here[:, :, 4:5, :], here[:, :, 5:6, :]

    lax.fori_loop(0, count, one, (zero, zero, zero, zero))


def columns_x(spike_t, inverse):
    sub, lane = iota((N, N), 0), iota((N, N), 1)
    turn = lane % 32
    outer = jnp.dot(inverse, outer_stencil(sub, turn // 4, 2), precision=HIGH, preferred_element_type=F32)
    order = sub % 32 // 4
    spikes = jnp.where(order == 0, spike_t[0:1], jnp.where(order == 1, spike_t[1:2], 0.0)).T
    return outer + spikes


def columns_y(spike_t, inverse):
    sub, lane = iota((N, N), 0), iota((N, N), 1)
    outer = jnp.dot(inverse, outer_stencil(sub, lane % 8, 2), precision=HIGH, preferred_element_type=F32)
    order = sub % 8
    spikes = jnp.where(order == 0, spike_t[0:1], jnp.where(order == 1, spike_t[1:2], 0.0)).T
    return outer + spikes


def inner(inverse):
    sub, lane = iota((N, N), 0), iota((N, N), 1)
    return jnp.dot(inverse, inner_stencil(lane, sub), precision=HIGH, preferred_element_type=F32)


def chain_x(count, got, reply):
    real = iota((1, 4, N), 1) < 3
    zero = jnp.zeros((got.shape[1], 4, N), F32)

    def one(d, carry):
        s0, s1 = carry
        here = got[d]
        reply[d] = jnp.concatenate([s0, s1], axis=1)
        new = []
        for a in range(2):
            weight = here[0:1, 4 * a + 3 : 4 * a + 4, :]
            part = jnp.where(real, here[:, 4 * a : 4 * a + 4, :], 0.0)
            new.append(part + weight[:, :, 4:5] * s0 + weight[:, :, 5:6] * s1)
        return tuple(new)

    lax.fori_loop(0, count, one, (zero, zero))


def whole_kernel(nx, ny, v_hbm, ix_hbm, iy_hbm, wx_hbm, wy_hbm, f_hbm, k_hbm, own_hbm, row_hbm, out_ref,
                 v_ref, ix_ref, iy_ref, wx_ref, wy_ref, f_ref, k_ref, own_ref, row_ref, load_sem,
                 wide_ref, pos_ref, mk_ref, got_mk, qx_ref, my_ref, line_ref,
                 edge_ref, low_ref, high_ref, ex_ref, ey_ref, got_x, got_y, reply_x, reply_y,
                 tile_ref, pick_ref, left_x, left_ex, right_y, right_ey, ext_y,
                 send_m, recv_m, send_x, recv_x, send_y, recv_y,
                 back_send_x, back_recv_x, back_send_y, back_recv_y, edge_send, edge_recv):
    gx, gy = lax.axis_index("gx"), lax.axis_index("gy")
    depth = v_ref.shape[1]
    half = depth // 2
    sx, sy = min(depth, nx), min(depth, ny)
    zx, zy = depth // sx, depth // sy
    chunks = own_ref.shape[0]
    per = 4
    rounds = nx // per
    sub, lane = iota((N, N), 0), iota((N, N), 1)

    pairs = [(own_hbm, own_ref), (row_hbm, row_ref), (f_hbm, f_ref), (k_hbm, k_ref), (v_hbm, v_ref),
             (ix_hbm, ix_ref), (iy_hbm, iy_ref), (wx_hbm, wx_ref), (wy_hbm, wy_ref)]
    loads = [pltpu.make_async_copy(src, dst, load_sem.at[i]) for i, (src, dst) in enumerate(pairs)]
    for load in loads:
        load.start()

    barrier = pltpu.get_barrier_semaphore()

    @pl.loop(1, nx)
    def _(i):
        pl.semaphore_signal(barrier, inc=1, device_id=(lax.rem(gx + i, nx), gy), device_id_type=MESH)

    @pl.loop(1, ny)
    def _(i):
        pl.semaphore_signal(barrier, inc=1, device_id=(gx, lax.rem(gy + i, ny)), device_id_type=MESH)

    def remote(src, dst, send, recv, to):
        return pltpu.make_async_remote_copy(
            src_ref=src, dst_ref=dst, send_sem=send, recv_sem=recv, device_id=to, device_id_type=MESH)

    def out_x(to, origin):
        return remote(qx_ref.at[pl.ds(to * zx, zx)], got_x.at[origin], send_x.at[to], recv_x.at[origin], (to, gy))

    def out_y(to, origin):
        return remote(my_ref.at[pl.ds(to * zy, zy)], got_y.at[origin], send_y.at[to], recv_y.at[origin], (gx, to))

    def out_m(to, origin):
        return remote(mk_ref.at[to], got_mk.at[origin], send_m.at[to], recv_m.at[origin], (to, gy))

    def back_x(to, origin):
        return remote(reply_x.at[to], ex_ref.at[pl.ds(origin * zx, zx)], back_send_x.at[to], back_recv_x.at[origin], (to, gy))

    def back_y(to, origin):
        return remote(reply_y.at[to], ey_ref.at[pl.ds(origin * zy, zy)], back_send_y.at[to], back_recv_y.at[origin], (gx, to))

    def edge_low():
        return remote(edge_ref.at[1], low_ref, edge_send.at[0], edge_recv.at[0], (jnp.minimum(gx + 1, nx - 1), gy))

    def edge_high():
        return remote(edge_ref.at[0], high_ref, edge_send.at[1], edge_recv.at[1], (jnp.maximum(gx - 1, 0), gy))

    for load in loads[:4]:
        load.wait()
    upto = jnp.concatenate([(sub <= lane).astype(BF16), jnp.ones((N, N), BF16)], axis=1)
    name = iota((nx, N), 0)
    before = jnp.zeros((nx, N), F32)
    for k in range(chunks):
        owner = own_ref[k : k + 1, :]
        hit = name == owner
        counted = mm(hit.astype(F32).astype(BF16), upto)
        rank = counted[:, :N] + before - 1.0
        before = before + counted[:, N:]
        place = jnp.sum(jnp.where(hit, rank, 0.0), axis=0, keepdims=True)
        pos_ref[0:1, k * N : (k + 1) * N] = owner.astype(F32)
        pos_ref[1:2, k * N : (k + 1) * N] = place

        cell = row_ref[k : k + 1, :]
        plane = cell // N
        upper = plane >= half
        three = f_ref[:, k * N : (k + 1) * N].astype(F32)
        facts = jnp.concatenate(
            [jnp.where(upper, 0.0, three), jnp.where(upper, three, 0.0),
             (plane % half).astype(F32), (cell % N).astype(F32)],
            axis=0,
        )
        wide_ref[k * N : (k + 1) * N, 0:N] = k_ref[k * N : (k + 1) * N, :]
        wide_ref[k * N : (k + 1) * N, N:] = jnp.tile(facts, (N // 8, 1)).T.astype(BF16)

    for load in loads[4:]:
        load.wait()
    blank = jnp.zeros((depth, 1, N), F32)
    for e, first in enumerate((0, N - 2)):
        edge_ref[e] = jnp.concatenate(
            [p for a in range(2) for p in [v_ref[c, :, first + a : first + a + 1, :] for c in range(3)] + [blank]], axis=1)

    pl.semaphore_wait(barrier, nx + ny - 2)

    @pl.when(gx < nx - 1)
    def _():
        edge_low().start()

    @pl.when(gx > 0)
    def _():
        edge_high().start()

    slot = iota((CAP, 1), 0).astype(F32).astype(BF16)

    def compact(low, high):
        @pl.loop(low, high)
        def _(step):
            owner, place = pos_ref[0:1, :], pos_ref[1:2, :]
            picks = []
            for i in range(per):
                to = lax.rem(gx + step * per + i, nx)
                mine = jnp.where(owner == to.astype(F32), place, -1.0).astype(BF16)
                picks.append(jnp.where(mine == slot, jnp.ones((), BF16), jnp.zeros((), BF16)))
            rows = mm(jnp.concatenate(picks, axis=0), wide_ref[...])
            for i in range(per):
                off = step * per + i
                to = lax.rem(gx + off, nx)
                part = rows[i * CAP : (i + 1) * CAP]
                mk_ref[to, 0:CAP, :] = part[:, :N].astype(BF16)
                facts_t = part[:, N:].T[0:8, :]
                mk_ref[to, CAP:, :] = jnp.concatenate([facts_t, jnp.zeros((8, N), F32)], axis=0).astype(BF16)

                @pl.when(off > 0)
                def _():
                    out_m(to, gx).start()

                @pl.when(off == 0)
                def _():
                    got_mk[gx] = mk_ref[gx]

    cuts = (0, rounds // 4, 5 * rounds // 8, rounds)
    compact(cuts[0], cuts[1])

    (sy0, sy1), (cy0, cy1) = last_rows(iy_ref[...], wy_ref[...])
    kind = lane % 8
    base = jnp.where(kind == 0, sy0, jnp.where(kind == 1, sy1, 0.0))
    for i, cell in enumerate((0, 1, N - 2, N - 1)):
        base = base + jnp.where((kind == 2 + i) & (sub == cell), 1.0, 0.0)
    base_hi, base_lo = (p.astype(F32) for p in split(base))
    line_ref[...] = jnp.zeros_like(line_ref)

    @pl.loop(0, depth)
    def _(z):
        mine = lane // 8 == z
        hi = jnp.where(mine, base_hi, 0.0).astype(BF16)
        lo = jnp.where(mine, base_lo, 0.0).astype(BF16)
        v_hi, v_lo = split(v_ref[:, z].reshape(3 * N, N))
        line_ref[...] += mm(jnp.concatenate([v_hi, v_lo], axis=1), jnp.concatenate([hi, hi], axis=0)) + mm(v_hi, lo)

    kind_row = sub % 8
    for c in range(3):
        lines = line_ref[c * N : (c + 1) * N, :].T
        lines = jnp.where(kind_row == 6, cy0, jnp.where(kind_row == 7, cy1, lines))
        my_ref[:, c] = lines.reshape(depth, 8, N)

    @pl.loop(1, ny)
    def _(i):
        out_y(lax.rem(gy + i, ny), gy).start()

    (sx0, sx1), (cx0, cx1) = last_rows(ix_ref[...], wx_ref[...])

    @pl.loop(0, depth)
    def _(z):
        rows = []
        for weight, known in ((sx0, cx0), (sx1, cx1)):
            rows += [jnp.sum(v_ref[c, z] * weight, axis=0, keepdims=True) for c in range(3)] + [known]
        qx_ref[z] = jnp.concatenate(rows, axis=0)

    @pl.when(gx == 0)
    def _():
        low_ref[...] = jnp.zeros_like(low_ref)

    @pl.when(gx == nx - 1)
    def _():
        high_ref[...] = jnp.zeros_like(high_ref)

    @pl.when(gx > 0)
    def _():
        edge_low().wait_recv()

    @pl.when(gx < nx - 1)
    def _():
        edge_high().wait_recv()

    outer = [low_ref[:, 0:4], low_ref[:, 4:8], high_ref[:, 0:4], high_ref[:, 4:8]]
    for a, known in ((0, cx0), (1, cx1)):
        total = qx_ref[:, 4 * a : 4 * a + 4]
        for k in range(4):
            total = total + known[:, k : k + 1].reshape(1, 1, 1) * outer[k]
        qx_ref[:, 4 * a : 4 * a + 4] = total

    @pl.loop(0, sx)
    def _(i):
        to = lax.rem(gx + i, sx)

        @pl.when(to != gx)
        def _():
            out_x(to, gx).start()

    compact(cuts[1], cuts[2])

    got_y[gy] = my_ref[pl.ds(gy * zy, zy)]

    @pl.loop(1, ny)
    def _(i):
        out_y(gy, lax.rem(gy + i, ny)).wait_recv()

    chain_y(ny, got_y, reply_y)

    @pl.loop(1, ny)
    def _(i):
        back_y(lax.rem(gy + i, ny), gy).start()

    ey_ref[pl.ds(gy * zy, zy)] = reply_y[gy]

    @pl.when(gx < sx)
    def _():
        got_x[gx] = qx_ref[pl.ds(gx * zx, zx)]

        @pl.loop(1, nx)
        def _(i):
            out_x(gx, lax.rem(gx + i, nx)).wait_recv()

        chain_x(nx, got_x, reply_x)

        @pl.loop(1, nx)
        def _(i):
            back_x(lax.rem(gx + i, nx), gx).start()

        ex_ref[pl.ds(gx * zx, zx)] = reply_x[gx]

    compact(cuts[2], cuts[3])

    out_ref[...] = jnp.zeros_like(out_ref)
    hi, lo = split(inner(ix_ref[...]))
    left_x[0:N, 0:N], left_x[0:N, N:] = hi, hi
    left_x[N:, 0:N], left_x[N:, N:] = lo, lo
    cols = columns_x(wx_ref[...], ix_ref[...])
    for c in range(3):
        hi, lo = split(jnp.where(lane % 4 == c, cols, 0.0))
        left_ex[2 * c * N : (2 * c + 1) * N], left_ex[(2 * c + 1) * N : (2 * c + 2) * N] = hi, lo
    hi, lo = split(inner(iy_ref[...]).T)
    right_y[0:N, 0:N], right_y[0:N, N:] = hi, lo
    right_y[N:, 0:N], right_y[N:, N:] = hi, lo
    hi, lo = split(columns_y(wy_ref[...], iy_ref[...]).T)
    right_ey[0:N, 0:N], right_ey[0:N, N:] = hi, lo
    right_ey[N:, 0:N], right_ey[N:, N:] = hi, lo

    def scatter(low, high):
        @pl.loop(low, high)
        def _(step):
            facts = []
            for i in range(per):
                off = step * per + i
                source = lax.rem(gx + nx - off, nx)

                @pl.when(off > 0)
                def _():
                    out_m(gx, source).wait_recv()

                facts.append(got_mk[source, CAP:, :].astype(F32)[0:8])
            stack = jnp.concatenate(facts, axis=0)
            columns = jnp.tile(stack, (N // (8 * per), 1)).T
            for i in range(per):
                source = lax.rem(gx + nx - (step * per + i), nx)
                rows = got_mk[source, 0:CAP, :].astype(F32)
                for k in range(6):
                    tile_ref[i * CAP : (i + 1) * CAP, k * N : (k + 1) * N] = (rows * columns[:, 8 * i + k : 8 * i + k + 1]).astype(BF16)
                for zz in range(half):
                    mine = jnp.where(facts[i][6:7] == float(zz), facts[i][7:8], -1.0).astype(BF16)
                    pick_ref[zz * N : (zz + 1) * N, i * CAP : (i + 1) * CAP] = jnp.where(
                        mine == slot, jnp.ones((), BF16), jnp.zeros((), BF16))
            for h in range(2):
                for r in range(2):
                    count = half // 2
                    more = mm(pick_ref[r * count * N : (r + 1) * count * N, :], tile_ref[:, h * 3 * N : (h + 1) * 3 * N])
                    for c in range(3):
                        at = slice(h * half + r * count, h * half + (r + 1) * count)
                        out_ref[c, at] += 0.5 * more[:, c * N : (c + 1) * N].reshape(count, N, N)

    scatter(0, cuts[2])

    @pl.loop(1, ny)
    def _(i):
        back_y(gy, lax.rem(gy + i, ny)).wait_recv()

    @pl.loop(0, sx)
    def _(i):
        other = lax.rem(gx + i, sx)

        @pl.when(other != gx)
        def _():
            back_x(gx, other).wait_recv()

    for c in range(3):
        hi, lo = split(ey_ref[:, c].reshape(8 * depth, N).T)
        ext_y[c * N : (c + 1) * N, 0:N], ext_y[c * N : (c + 1) * N, N:] = hi, lo

    @pl.loop(0, half)
    def _(step):
        zs = [step, step + half]
        vs = [[v_ref[c, z] for c in range(3)] for z in zs]
        parts = [[split(v) for v in line] for line in vs]
        wide = jnp.concatenate([jnp.concatenate([hi, lo], axis=0) for line in parts for hi, lo in line], axis=1)
        both = mm(left_x[...], wide)
        ends = []
        for z in zs:
            hi, lo = split(jnp.concatenate([ex_ref[z], low_ref[z], high_ref[z], jnp.zeros((8, N), F32)], axis=0))
            ends.append(jnp.concatenate([hi, lo], axis=0))
        bent = mm(left_ex[:, 0:64], jnp.concatenate(ends, axis=1))
        for h, z in enumerate(zs):
            tall = jnp.concatenate([jnp.concatenate([hi, lo], axis=1) for hi, lo in parts[h]], axis=0)
            mine = iota((2 * N, 2 * N), 0) % N // 8 == z
            right_ext = jnp.where(mine, right_ey[...].astype(F32), 0.0).astype(BF16)
            across = mm(tall, right_y[...]) + mm(ext_y[...], right_ext)
            for c in range(3):
                k = h * 3 + c
                dx = both[:N, k * N : (k + 1) * N] + both[N:, k * N : (k + 1) * N]
                dx = dx + bent[2 * c * N : (2 * c + 1) * N, h * N : (h + 1) * N] + bent[(2 * c + 1) * N : (2 * c + 2) * N, h * N : (h + 1) * N]
                dy = across[c * N : (c + 1) * N, :N] + across[c * N : (c + 1) * N, N:]
                out_ref[c, z] += vs[h][c] - 0.5 * (vs[h][0] * dx + vs[h][1] * dy)

    scatter(cuts[2], cuts[3])

    @pl.loop(1, ny)
    def _(i):
        other = lax.rem(gy + i, ny)
        out_y(other, gy).wait_send()
        back_y(other, gy).wait_send()

    @pl.loop(0, sx)
    def _(i):
        other = lax.rem(gx + i, sx)

        @pl.when(other != gx)
        def _():
            out_x(other, gx).wait_send()

    @pl.when(gx < sx)
    def _():
        @pl.loop(1, nx)
        def _(i):
            back_x(lax.rem(gx + i, nx), gx).wait_send()

    @pl.loop(1, nx)
    def _(i):
        out_m(lax.rem(gx + i, nx), gx).wait_send()

    @pl.when(gx < nx - 1)
    def _():
        edge_low().wait_send()

    @pl.when(gx > 0)
    def _():
        edge_high().wait_send()


def local(nx, ny, velocity, inv_x, inv_y, spike_x, spike_y, marker_force, marker_kernel, marker_owner, marker_row):
    depth = velocity.shape[1]
    half = depth // 2
    slots = marker_row.shape[0]
    args = (velocity, inv_x, inv_y, spike_x.T, spike_y.T, marker_force, marker_kernel,
            marker_owner.reshape(slots // N, N), marker_row.reshape(slots // N, N))
    sx, sy = min(depth, nx), min(depth, ny)
    dma, vmem = pltpu.SemaphoreType.DMA, pltpu.VMEM
    return pl.pallas_call(
        functools.partial(whole_kernel, nx, ny),
        out_shape=jax.ShapeDtypeStruct(velocity.shape, F32),
        in_specs=[pl.BlockSpec(memory_space=pl.ANY)] * len(args),
        out_specs=pl.BlockSpec(memory_space=pltpu.VMEM),
        scratch_shapes=[vmem(a.shape, a.dtype) for a in args] + [
            dma((len(args),)),
            vmem((slots, 2 * N), BF16),
            vmem((8, slots), F32),
            vmem((nx, BLOCK, N), BF16),
            vmem((nx, BLOCK, N), BF16),
            vmem((depth, 8, N), F32),
            vmem((depth, 3, 8, N), F32),
            vmem((3 * N, N), F32),
            vmem((2, depth, 8, N), F32),
            vmem((depth, 8, N), F32),
            vmem((depth, 8, N), F32),
            vmem((depth, 8, N), F32),
            vmem((depth, 3, 8, N), F32),
            vmem((nx, depth // sx, 8, N), F32),
            vmem((ny, depth // sy, 3, 8, N), F32),
            vmem((nx, depth // sx, 8, N), F32),
            vmem((ny, depth // sy, 3, 8, N), F32),
            vmem((4 * CAP, 6 * N), BF16),
            vmem((half * N, 4 * CAP), BF16),
            vmem((2 * N, 2 * N), BF16),
            vmem((6 * N, N), BF16),
            vmem((2 * N, 2 * N), BF16),
            vmem((2 * N, 2 * N), BF16),
            vmem((3 * N, 2 * N), BF16),
            dma((nx,)), dma((nx,)), dma((sx,)), dma((nx,)), dma((ny,)), dma((ny,)),
            dma((nx,)), dma((sx,)), dma((ny,)), dma((ny,)), dma((2,)), dma((2,)),
        ],
        compiler_params=pltpu.CompilerParams(vmem_limit_bytes=56 * 1024 * 1024, collective_id=0, has_side_effects=True),
        name="section",
    )(*args)


def solution(mesh):
    return jax.shard_map(
        functools.partial(local, mesh.shape["gx"], mesh.shape["gy"]),
        mesh=mesh,
        in_specs=(
            P(None, None, "gx", "gy"),
            P("gx", None),
            P("gy", None),
            P("gx", None),
            P("gy", None),
            P(None, ("gx", "gy")),
            P(("gx", "gy"), None),
            P(("gx", "gy"), None),
            P(("gx", "gy")),
        ),
        out_specs=P(None, None, "gx", "gy"),
        check_vma=False,
    )
```

profile of v0, /device:TPU:1, one launch (start us, length us, event | category | flops | bytes accessed | tf_op | source)
XLA Modules:
  0.0 57.2 jit_solution(5683587019378939364)
XLA Ops:
  0.0 53.2 %section.1 = f32[3,16,128,128]{3,2,1,0:T(8,128)} custom-call(f32[3,16,128,128]{3,2,1,0:T(8,128)} %v_hbm.1, f32[128,128]{1,0:T(8,128)} %ix_hbm.1, f32[128,128]{1,0:T(8,128)} %iy_hbm.1, f32[2,128]{1,0:T(2,128)} %bitcast.6, f32[2,128]{1,0:T(2,128)} %bitcast.7, bf16[3,2048]{1,0:T(4,128)(2,1)} %f_hbm.1, bf16[2048,128]{1,0:T(8,128)(2,1)} %k_hbm.1, ...), custom_call_target="tpu_custom_call" | custom-call | tf_op jit(solution)/shard_map/section/pallas_call | solution.py:497
  53.2 3.9 %copy.11 = f32[3,16,128,128]{3,2,1,0:T(8,128)} copy(f32[3,16,128,128]{3,2,1,0:T(8,128)} %section.1) | data formatting | bytes 6291456
where the time goes:
time: 57.8 us; the launch traced here: 57.2 us
  Pallas kernels  53.2 us (92%)
  local copies, waits for them, and re-layouts  3.91 us (7%)
    pallas_call x1, Pallas kernels, local(): pl.pallas_call(functools.partial(whole_kernel, nx, ny), out_shape=jax.Sha...  53.2 us
    unnamed x1, local copies, waits for them, and re-layouts  3.91 us

commit v1 on v0

--- a/solution.py
+++ b/solution.py
@@ -86,7 +86,7 @@
             new.append(total)
         return new[0], new[1], here[:, :, 4:5, :], here[:, :, 5:6, :]
 
-    lax.fori_loop(0, count, one, (zero, zero, zero, zero))
+    lax.fori_loop(0, count, one, (zero, zero, zero, zero), unroll=2)
 
 
 def columns_x(spike_t, inverse):
@@ -126,16 +126,16 @@
             new.append(part + weight[:, :, 4:5] * s0 + weight[:, :, 5:6] * s1)
         return tuple(new)
 
-    lax.fori_loop(0, count, one, (zero, zero))
-
-
-def whole_kernel(nx, ny, v_hbm, ix_hbm, iy_hbm, wx_hbm, wy_hbm, f_hbm, k_hbm, own_hbm, row_hbm, out_ref,
+    lax.fori_loop(0, count, one, (zero, zero), unroll=min(count, 8))
+
+
+def whole_kernel(nx, ny, v_hbm, ix_hbm, iy_hbm, wx_hbm, wy_hbm, f_hbm, k_hbm, own_hbm, row_hbm, out_hbm,
                  v_ref, ix_ref, iy_ref, wx_ref, wy_ref, f_ref, k_ref, own_ref, row_ref, load_sem,
                  wide_ref, pos_ref, mk_ref, got_mk, qx_ref, my_ref, line_ref,
                  edge_ref, low_ref, high_ref, ex_ref, ey_ref, got_x, got_y, reply_x, reply_y,
                  tile_ref, pick_ref, left_x, left_ex, right_y, right_ey, ext_y,
                  send_m, recv_m, send_x, recv_x, send_y, recv_y,
-                 back_send_x, back_recv_x, back_send_y, back_recv_y, edge_send, edge_recv):
+                 back_send_x, back_recv_x, back_send_y, back_recv_y, edge_send, edge_recv, out_ref, store_sem):
     gx, gy = lax.axis_index("gx"), lax.axis_index("gy")
     depth = v_ref.shape[1]
     half = depth // 2
@@ -259,7 +259,7 @@
                 def _():
                     got_mk[gx] = mk_ref[gx]
 
-    cuts = (0, rounds // 4, 5 * rounds // 8, rounds)
+    cuts = (0, max(1, rounds // 4), max(1, 3 * rounds // 4), rounds)
     compact(cuts[0], cuts[1])
 
     (sy0, sy1), (cy0, cy1) = last_rows(iy_ref[...], wy_ref[...])
@@ -330,39 +330,52 @@
 
     compact(cuts[1], cuts[2])
 
-    got_y[gy] = my_ref[pl.ds(gy * zy, zy)]
-
-    @pl.loop(1, ny)
-    def _(i):
-        out_y(gy, lax.rem(gy + i, ny)).wait_recv()
-
-    chain_y(ny, got_y, reply_y)
-
-    @pl.loop(1, ny)
-    def _(i):
-        back_y(lax.rem(gy + i, ny), gy).start()
-
-    ey_ref[pl.ds(gy * zy, zy)] = reply_y[gy]
-
-    @pl.when(gx < sx)
-    def _():
-        got_x[gx] = qx_ref[pl.ds(gx * zx, zx)]
-
-        @pl.loop(1, nx)
-        def _(i):
-            out_x(gx, lax.rem(gx + i, nx)).wait_recv()
-
-        chain_x(nx, got_x, reply_x)
-
-        @pl.loop(1, nx)
-        def _(i):
-            back_x(lax.rem(gx + i, nx), gx).start()
-
-        ex_ref[pl.ds(gx * zx, zx)] = reply_x[gx]
-
-    compact(cuts[2], cuts[3])
-
+    many = nx // 4
+    choice = jnp.full((), 0.5, BF16)
     out_ref[...] = jnp.zeros_like(out_ref)
+
+    def stores(h, r):
+        count = half // 2
+        at = pl.ds(h * half + r * count, count)
+        return [pltpu.make_async_copy(out_ref.at[c, at], out_hbm.at[c, at], store_sem.at[6 * h + 3 * r + c]) for c in range(3)]
+
+    def scatter_one(step, last):
+        facts = []
+        for i in range(many):
+            off = step * many + i
+            source = lax.rem(gx + nx - off, nx)
+
+            @pl.when(off > 0)
+            def _():
+                out_m(gx, source).wait_recv()
+
+            facts.append(got_mk[source, CAP:, :].astype(F32)[0:8])
+        stack = jnp.concatenate(facts, axis=0)
+        columns = jnp.tile(stack, (N // (8 * many), 1)).T.astype(BF16)
+        for i in range(many):
+            source = lax.rem(gx + nx - (step * many + i), nx)
+            rows = got_mk[source, 0:CAP, :]
+            for k in range(6):
+                tile_ref[i * CAP : (i + 1) * CAP, k * N : (k + 1) * N] = rows * columns[:, 8 * i + k : 8 * i + k + 1]
+            for zz in range(half):
+                mine = jnp.where(facts[i][6:7] == float(zz), facts[i][7:8], -1.0).astype(BF16)
+                pick_ref[zz * N : (zz + 1) * N, i * CAP : (i + 1) * CAP] = jnp.where(mine == slot, choice, jnp.zeros((), BF16))
+        for h in range(2):
+            for r in range(2):
+                count = half // 2
+                more = mm(pick_ref[r * count * N : (r + 1) * count * N, :], tile_ref[:, h * 3 * N : (h + 1) * 3 * N])
+                for c in range(3):
+                    at = slice(h * half + r * count, h * half + (r + 1) * count)
+                    out_ref[c, at] += more[:, c * N : (c + 1) * N].reshape(count, N, N)
+                if last:
+                    for store in stores(h, r):
+                        store.start()
+
+    def scatter(low, high):
+        @pl.loop(low, high)
+        def _(step):
+            scatter_one(step, False)
+
     hi, lo = split(inner(ix_ref[...]))
     left_x[0:N, 0:N], left_x[0:N, N:] = hi, hi
     left_x[N:, 0:N], left_x[N:, N:] = lo, lo
@@ -377,39 +390,41 @@
     right_ey[0:N, 0:N], right_ey[0:N, N:] = hi, lo
     right_ey[N:, 0:N], right_ey[N:, N:] = hi, lo
 
-    def scatter(low, high):
-        @pl.loop(low, high)
-        def _(step):
-            facts = []
-            for i in range(per):
-                off = step * per + i
-                source = lax.rem(gx + nx - off, nx)
-
-                @pl.when(off > 0)
-                def _():
-                    out_m(gx, source).wait_recv()
-
-                facts.append(got_mk[source, CAP:, :].astype(F32)[0:8])
-            stack = jnp.concatenate(facts, axis=0)
-            columns = jnp.tile(stack, (N // (8 * per), 1)).T
-            for i in range(per):
-                source = lax.rem(gx + nx - (step * per + i), nx)
-                rows = got_mk[source, 0:CAP, :].astype(F32)
-                for k in range(6):
-                    tile_ref[i * CAP : (i + 1) * CAP, k * N : (k + 1) * N] = (rows * columns[:, 8 * i + k : 8 * i + k + 1]).astype(BF16)
-                for zz in range(half):
-                    mine = jnp.where(facts[i][6:7] == float(zz), facts[i][7:8], -1.0).astype(BF16)
-                    pick_ref[zz * N : (zz + 1) * N, i * CAP : (i + 1) * CAP] = jnp.where(
-                        mine == slot, jnp.ones((), BF16), jnp.zeros((), BF16))
-            for h in range(2):
-                for r in range(2):
-                    count = half // 2
-                    more = mm(pick_ref[r * count * N : (r + 1) * count * N, :], tile_ref[:, h * 3 * N : (h + 1) * 3 * N])
-                    for c in range(3):
-                        at = slice(h * half + r * count, h * half + (r + 1) * count)
-                        out_ref[c, at] += 0.5 * more[:, c * N : (c + 1) * N].reshape(count, N, N)
-
-    scatter(0, cuts[2])
+    scatter(0, 1)
+
+    got_y[gy] = my_ref[pl.ds(gy * zy, zy)]
+
+    @pl.loop(1, ny)
+    def _(i):
+        out_y(gy, lax.rem(gy + i, ny)).wait_recv()
+
+    chain_y(ny, got_y, reply_y)
+
+    @pl.loop(1, ny)
+    def _(i):
+        back_y(lax.rem(gy + i, ny), gy).start()
+
+    ey_ref[pl.ds(gy * zy, zy)] = reply_y[gy]
+
+    @pl.when(gx < sx)
+    def _():
+        got_x[gx] = qx_ref[pl.ds(gx * zx, zx)]
+
+        @pl.loop(1, nx)
+        def _(i):
+            out_x(gx, lax.rem(gx + i, nx)).wait_recv()
+
+        chain_x(nx, got_x, reply_x)
+
+        @pl.loop(1, nx)
+        def _(i):
+            back_x(lax.rem(gx + i, nx), gx).start()
+
+        ex_ref[pl.ds(gx * zx, zx)] = reply_x[gx]
+
+    compact(cuts[2], cuts[3])
+
+    scatter(1, nx // many - 1)
 
     @pl.loop(1, ny)
     def _(i):
@@ -451,7 +466,7 @@
                 dy = across[c * N : (c + 1) * N, :N] + across[c * N : (c + 1) * N, N:]
                 out_ref[c, z] += vs[h][c] - 0.5 * (vs[h][0] * dx + vs[h][1] * dy)
 
-    scatter(cuts[2], cuts[3])
+    scatter_one(nx // many - 1, True)
 
     @pl.loop(1, ny)
     def _(i):
@@ -484,6 +499,24 @@
     @pl.when(gx > 0)
     def _():
         edge_high().wait_send()
+
+    for h in range(2):
+        for r in range(2):
+            for store in stores(h, r):
+                store.wait()
+
+
+def finish_kernel(src, dst, held, load_sem, store_sem):
+    spots = [(c, pl.ds(4 * i, 4)) for c in range(3) for i in range(4)]
+    loads = [pltpu.make_async_copy(src.at[p], held.at[p], load_sem.at[i]) for i, p in enumerate(spots)]
+    stores = [pltpu.make_async_copy(held.at[p], dst.at[p], store_sem.at[i]) for i, p in enumerate(spots)]
+    for load in loads:
+        load.start()
+    for load, store in zip(loads, stores):
+        load.wait()
+        store.start()
+    for store in stores:
+        store.wait()
 
 
 def local(nx, ny, velocity, inv_x, inv_y, spike_x, spike_y, marker_force, marker_kernel, marker_owner, marker_row):
@@ -494,11 +527,11 @@
             marker_owner.reshape(slots // N, N), marker_row.reshape(slots // N, N))
     sx, sy = min(depth, nx), min(depth, ny)
     dma, vmem = pltpu.SemaphoreType.DMA, pltpu.VMEM
-    return pl.pallas_call(
+    result = pl.pallas_call(
         functools.partial(whole_kernel, nx, ny),
         out_shape=jax.ShapeDtypeStruct(velocity.shape, F32),
         in_specs=[pl.BlockSpec(memory_space=pl.ANY)] * len(args),
-        out_specs=pl.BlockSpec(memory_space=pltpu.VMEM),
+        out_specs=pl.BlockSpec(memory_space=pl.ANY),
         scratch_shapes=[vmem(a.shape, a.dtype) for a in args] + [
             dma((len(args),)),
             vmem((slots, 2 * N), BF16),
@@ -517,8 +550,8 @@
             vmem((ny, depth // sy, 3, 8, N), F32),
             vmem((nx, depth // sx, 8, N), F32),
             vmem((ny, depth // sy, 3, 8, N), F32),
-            vmem((4 * CAP, 6 * N), BF16),
-            vmem((half * N, 4 * CAP), BF16),
+            vmem((nx // 4 * CAP, 6 * N), BF16),
+            vmem((half * N, nx // 4 * CAP), BF16),
             vmem((2 * N, 2 * N), BF16),
             vmem((6 * N, N), BF16),
             vmem((2 * N, 2 * N), BF16),
@@ -526,10 +559,20 @@
             vmem((3 * N, 2 * N), BF16),
             dma((nx,)), dma((nx,)), dma((sx,)), dma((nx,)), dma((ny,)), dma((ny,)),
             dma((nx,)), dma((sx,)), dma((ny,)), dma((ny,)), dma((2,)), dma((2,)),
+            vmem(velocity.shape, F32), dma((12,)),
         ],
         compiler_params=pltpu.CompilerParams(vmem_limit_bytes=56 * 1024 * 1024, collective_id=0, has_side_effects=True),
         name="section",
     )(*args)
+    return pl.pallas_call(
+        finish_kernel,
+        out_shape=jax.ShapeDtypeStruct(velocity.shape, F32),
+        in_specs=[pl.BlockSpec(memory_space=pl.ANY)],
+        out_specs=pl.BlockSpec(memory_space=pl.ANY),
+        scratch_shapes=[vmem(velocity.shape, F32), dma((12,)), dma((12,))],
+        compiler_params=pltpu.CompilerParams(vmem_limit_bytes=60 * 1024 * 1024),
+        name="finish",
+    )(result)
 
 
 def solution(mesh):

time: 57.8 us -> 51.7 us (0.89)
  local copies, waits for them, and re-layouts: 3.91 us -> 0 us
  Pallas kernels: 53.2 us -> 51.2 us
    pallas_call x1, Pallas kernels: 53.2 us -> 48.4 us  [local(): pl.pallas_call(functools.partial(whole_kernel, nx, ny), out_shape=jax.Sha...]
    unnamed x1 -> x0, local copies, waits for them, and re-layouts: 3.91 us -> none
    pallas_call x0 -> x1, Pallas kernels: none -> 2.81 us  [local(): pl.pallas_call(finish_kernel, out_shape=jax.ShapeDtypeStruct(velocity.sha...]
where the time goes in v1:
time: 51.7 us; the launch traced here: 51.4 us
  Pallas kernels  51.2 us (99%)
    pallas_call x1, Pallas kernels, local(): pl.pallas_call(functools.partial(whole_kernel, nx, ny), out_shape=jax.Sha...  48.4 us
    pallas_call x1, Pallas kernels, local(): pl.pallas_call(finish_kernel, out_shape=jax.ShapeDtypeStruct(velocity.sha...  2.81 us

profile of v1, /device:TPU:1, one launch (start us, length us, event | category | flops | bytes accessed | tf_op | source)
XLA Modules:
  0.0 51.4 jit_solution(12931353702129553078)
XLA Ops:
  0.0 48.4 %section.1.src = f32[3,16,128,128]{3,2,1,0:T(8,128)} custom-call(f32[3,16,128,128]{3,2,1,0:T(8,128)} %v_hbm.1, f32[128,128]{1,0:T(8,128)} %ix_hbm.1, f32[128,128]{1,0:T(8,128)} %iy_hbm.1, f32[2,128]{1,0:T(2,128)} %bitcast.6, f32[2,128]{1,0:T(2,128)} %bitcast.7, bf16[3,2048]{1,0:T(4,128)(2,1)} %f_hbm.1, bf16[2048,128]{1,0:T(8,128)(2,1)} %k_hbm.1, ...), custom_call_target="tpu_custom_call" | custom-call | tf_op jit(solution)/shard_map/section/pallas_call | solution.py:530
  48.4 2.8 %finish.1 = f32[3,16,128,128]{3,2,1,0:T(8,128)} custom-call(f32[3,16,128,128]{3,2,1,0:T(8,128)} %section.1.src), custom_call_target="tpu_custom_call" | custom-call | tf_op jit(solution)/shard_map/finish/pallas_call | solution.py:567

commit v2 on v1

--- a/solution.py
+++ b/solution.py
@@ -129,13 +129,13 @@
     lax.fori_loop(0, count, one, (zero, zero), unroll=min(count, 8))
 
 
-def whole_kernel(nx, ny, v_hbm, ix_hbm, iy_hbm, wx_hbm, wy_hbm, f_hbm, k_hbm, own_hbm, row_hbm, out_hbm,
+def whole_kernel(nx, ny, v_hbm, ix_hbm, iy_hbm, wx_hbm, wy_hbm, f_hbm, k_hbm, own_hbm, row_hbm, out_ref,
                  v_ref, ix_ref, iy_ref, wx_ref, wy_ref, f_ref, k_ref, own_ref, row_ref, load_sem,
                  wide_ref, pos_ref, mk_ref, got_mk, qx_ref, my_ref, line_ref,
                  edge_ref, low_ref, high_ref, ex_ref, ey_ref, got_x, got_y, reply_x, reply_y,
                  tile_ref, pick_ref, left_x, left_ex, right_y, right_ey, ext_y,
                  send_m, recv_m, send_x, recv_x, send_y, recv_y,
-                 back_send_x, back_recv_x, back_send_y, back_recv_y, edge_send, edge_recv, out_ref, store_sem):
+                 back_send_x, back_recv_x, back_send_y, back_recv_y, edge_send, edge_recv):
     gx, gy = lax.axis_index("gx"), lax.axis_index("gy")
     depth = v_ref.shape[1]
     half = depth // 2
@@ -330,19 +330,13 @@
 
     compact(cuts[1], cuts[2])
 
-    many = nx // 4
+    many, few = nx // 4, max(1, nx // 8)
     choice = jnp.full((), 0.5, BF16)
-    out_ref[...] = jnp.zeros_like(out_ref)
-
-    def stores(h, r):
-        count = half // 2
-        at = pl.ds(h * half + r * count, count)
-        return [pltpu.make_async_copy(out_ref.at[c, at], out_hbm.at[c, at], store_sem.at[6 * h + 3 * r + c]) for c in range(3)]
-
-    def scatter_one(step, last):
+
+    def scatter_one(first, many):
         facts = []
         for i in range(many):
-            off = step * many + i
+            off = first + i
             source = lax.rem(gx + nx - off, nx)
 
             @pl.when(off > 0)
@@ -353,7 +347,7 @@
         stack = jnp.concatenate(facts, axis=0)
         columns = jnp.tile(stack, (N // (8 * many), 1)).T.astype(BF16)
         for i in range(many):
-            source = lax.rem(gx + nx - (step * many + i), nx)
+            source = lax.rem(gx + nx - (first + i), nx)
             rows = got_mk[source, 0:CAP, :]
             for k in range(6):
                 tile_ref[i * CAP : (i + 1) * CAP, k * N : (k + 1) * N] = rows * columns[:, 8 * i + k : 8 * i + k + 1]
@@ -363,18 +357,15 @@
         for h in range(2):
             for r in range(2):
                 count = half // 2
-                more = mm(pick_ref[r * count * N : (r + 1) * count * N, :], tile_ref[:, h * 3 * N : (h + 1) * 3 * N])
+                more = mm(pick_ref[r * count * N : (r + 1) * count * N, 0 : many * CAP], tile_ref[0 : many * CAP, h * 3 * N : (h + 1) * 3 * N])
                 for c in range(3):
                     at = slice(h * half + r * count, h * half + (r + 1) * count)
                     out_ref[c, at] += more[:, c * N : (c + 1) * N].reshape(count, N, N)
-                if last:
-                    for store in stores(h, r):
-                        store.start()
 
     def scatter(low, high):
         @pl.loop(low, high)
         def _(step):
-            scatter_one(step, False)
+            scatter_one(step * many, many)
 
     hi, lo = split(inner(ix_ref[...]))
     left_x[0:N, 0:N], left_x[0:N, N:] = hi, hi
@@ -390,58 +381,6 @@
     right_ey[0:N, 0:N], right_ey[0:N, N:] = hi, lo
     right_ey[N:, 0:N], right_ey[N:, N:] = hi, lo
 
-    scatter(0, 1)
-
-    got_y[gy] = my_ref[pl.ds(gy * zy, zy)]
-
-    @pl.loop(1, ny)
-    def _(i):
-        out_y(gy, lax.rem(gy + i, ny)).wait_recv()
-
-    chain_y(ny, got_y, reply_y)
-
-    @pl.loop(1, ny)
-    def _(i):
-        back_y(lax.rem(gy + i, ny), gy).start()
-
-    ey_ref[pl.ds(gy * zy, zy)] = reply_y[gy]
-
-    @pl.when(gx < sx)
-    def _():
-        got_x[gx] = qx_ref[pl.ds(gx * zx, zx)]
-
-        @pl.loop(1, nx)
-        def _(i):
-            out_x(gx, lax.rem(gx + i, nx)).wait_recv()
-
-        chain_x(nx, got_x, reply_x)
-
-        @pl.loop(1, nx)
-        def _(i):
-            back_x(lax.rem(gx + i, nx), gx).start()
-
-        ex_ref[pl.ds(gx * zx, zx)] = reply_x[gx]
-
-    compact(cuts[2], cuts[3])
-
-    scatter(1, nx // many - 1)
-
-    @pl.loop(1, ny)
-    def _(i):
-        back_y(gy, lax.rem(gy + i, ny)).wait_recv()
-
-    @pl.loop(0, sx)
-    def _(i):
-        other = lax.rem(gx + i, sx)
-
-        @pl.when(other != gx)
-        def _():
-            back_x(gx, other).wait_recv()
-
-    for c in range(3):
-        hi, lo = split(ey_ref[:, c].reshape(8 * depth, N).T)
-        ext_y[c * N : (c + 1) * N, 0:N], ext_y[c * N : (c + 1) * N, N:] = hi, lo
-
     @pl.loop(0, half)
     def _(step):
         zs = [step, step + half]
@@ -449,24 +388,83 @@
         parts = [[split(v) for v in line] for line in vs]
         wide = jnp.concatenate([jnp.concatenate([hi, lo], axis=0) for line in parts for hi, lo in line], axis=1)
         both = mm(left_x[...], wide)
+        for h, z in enumerate(zs):
+            tall = jnp.concatenate([jnp.concatenate([hi, lo], axis=1) for hi, lo in parts[h]], axis=0)
+            across = mm(tall, right_y[...])
+            for c in range(3):
+                k = h * 3 + c
+                dx = both[:N, k * N : (k + 1) * N] + both[N:, k * N : (k + 1) * N]
+                dy = across[c * N : (c + 1) * N, :N] + across[c * N : (c + 1) * N, N:]
+                out_ref[c, z] = vs[h][c] - 0.5 * (vs[h][0] * dx + vs[h][1] * dy)
+
+    got_y[gy] = my_ref[pl.ds(gy * zy, zy)]
+
+    @pl.loop(1, ny)
+    def _(i):
+        out_y(gy, lax.rem(gy + i, ny)).wait_recv()
+
+    chain_y(ny, got_y, reply_y)
+
+    @pl.loop(1, ny)
+    def _(i):
+        back_y(lax.rem(gy + i, ny), gy).start()
+
+    ey_ref[pl.ds(gy * zy, zy)] = reply_y[gy]
+
+    @pl.when(gx < sx)
+    def _():
+        got_x[gx] = qx_ref[pl.ds(gx * zx, zx)]
+
+        @pl.loop(1, nx)
+        def _(i):
+            out_x(gx, lax.rem(gx + i, nx)).wait_recv()
+
+        chain_x(nx, got_x, reply_x)
+
+        @pl.loop(1, nx)
+        def _(i):
+            back_x(lax.rem(gx + i, nx), gx).start()
+
+        ex_ref[pl.ds(gx * zx, zx)] = reply_x[gx]
+
+    compact(cuts[2], cuts[3])
+
+    scatter(0, 3)
+
+    @pl.loop(1, ny)
+    def _(i):
+        back_y(gy, lax.rem(gy + i, ny)).wait_recv()
+
+    @pl.loop(0, sx)
+    def _(i):
+        other = lax.rem(gx + i, sx)
+
+        @pl.when(other != gx)
+        def _():
+            back_x(gx, other).wait_recv()
+
+    for c in range(3):
+        hi, lo = split(ey_ref[:, c].reshape(8 * depth, N).T)
+        ext_y[c * N : (c + 1) * N, 0:N], ext_y[c * N : (c + 1) * N, N:] = hi, lo
+
+    @pl.loop(0, half)
+    def _(step):
+        zs = [step, step + half]
         ends = []
         for z in zs:
             hi, lo = split(jnp.concatenate([ex_ref[z], low_ref[z], high_ref[z], jnp.zeros((8, N), F32)], axis=0))
             ends.append(jnp.concatenate([hi, lo], axis=0))
         bent = mm(left_ex[:, 0:64], jnp.concatenate(ends, axis=1))
         for h, z in enumerate(zs):
-            tall = jnp.concatenate([jnp.concatenate([hi, lo], axis=1) for hi, lo in parts[h]], axis=0)
             mine = iota((2 * N, 2 * N), 0) % N // 8 == z
-            right_ext = jnp.where(mine, right_ey[...].astype(F32), 0.0).astype(BF16)
-            across = mm(tall, right_y[...]) + mm(ext_y[...], right_ext)
+            across = mm(ext_y[...], jnp.where(mine, right_ey[...].astype(F32), 0.0).astype(BF16))
             for c in range(3):
-                k = h * 3 + c
-                dx = both[:N, k * N : (k + 1) * N] + both[N:, k * N : (k + 1) * N]
-                dx = dx + bent[2 * c * N : (2 * c + 1) * N, h * N : (h + 1) * N] + bent[(2 * c + 1) * N : (2 * c + 2) * N, h * N : (h + 1) * N]
+                dx = bent[2 * c * N : (2 * c + 1) * N, h * N : (h + 1) * N] + bent[(2 * c + 1) * N : (2 * c + 2) * N, h * N : (h + 1) * N]
                 dy = across[c * N : (c + 1) * N, :N] + across[c * N : (c + 1) * N, N:]
-                out_ref[c, z] += vs[h][c] - 0.5 * (vs[h][0] * dx + vs[h][1] * dy)
-
-    scatter_one(nx // many - 1, True)
+                out_ref[c, z] -= 0.5 * (v_ref[0, z] * dx + v_ref[1, z] * dy)
+
+    for first in range(3 * many, nx, few):
+        scatter_one(first, few)
 
     @pl.loop(1, ny)
     def _(i):
@@ -499,24 +497,6 @@
     @pl.when(gx > 0)
     def _():
         edge_high().wait_send()
-
-    for h in range(2):
-        for r in range(2):
-            for store in stores(h, r):
-                store.wait()
-
-
-def finish_kernel(src, dst, held, load_sem, store_sem):
-    spots = [(c, pl.ds(4 * i, 4)) for c in range(3) for i in range(4)]
-    loads = [pltpu.make_async_copy(src.at[p], held.at[p], load_sem.at[i]) for i, p in enumerate(spots)]
-    stores = [pltpu.make_async_copy(held.at[p], dst.at[p], store_sem.at[i]) for i, p in enumerate(spots)]
-    for load in loads:
-        load.start()
-    for load, store in zip(loads, stores):
-        load.wait()
-        store.start()
-    for store in stores:
-        store.wait()
 
 
 def local(nx, ny, velocity, inv_x, inv_y, spike_x, spike_y, marker_force, marker_kernel, marker_owner, marker_row):
@@ -527,11 +507,11 @@
             marker_owner.reshape(slots // N, N), marker_row.reshape(slots // N, N))
     sx, sy = min(depth, nx), min(depth, ny)
     dma, vmem = pltpu.SemaphoreType.DMA, pltpu.VMEM
-    result = pl.pallas_call(
+    return pl.pallas_call(
         functools.partial(whole_kernel, nx, ny),
-        out_shape=jax.ShapeDtypeStruct(velocity.shape, F32),
+        out_shape=vmem(velocity.shape, F32),
         in_specs=[pl.BlockSpec(memory_space=pl.ANY)] * len(args),
-        out_specs=pl.BlockSpec(memory_space=pl.ANY),
+        out_specs=pl.BlockSpec(memory_space=vmem),
         scratch_shapes=[vmem(a.shape, a.dtype) for a in args] + [
             dma((len(args),)),
             vmem((slots, 2 * N), BF16),
@@ -559,21 +539,10 @@
             vmem((3 * N, 2 * N), BF16),
             dma((nx,)), dma((nx,)), dma((sx,)), dma((nx,)), dma((ny,)), dma((ny,)),
             dma((nx,)), dma((sx,)), dma((ny,)), dma((ny,)), dma((2,)), dma((2,)),
-            vmem(velocity.shape, F32), dma((12,)),
         ],
         compiler_params=pltpu.CompilerParams(vmem_limit_bytes=56 * 1024 * 1024, collective_id=0, has_side_effects=True),
         name="section",
     )(*args)
-    return pl.pallas_call(
-        finish_kernel,
-        out_shape=jax.ShapeDtypeStruct(velocity.shape, F32),
-        in_specs=[pl.BlockSpec(memory_space=pl.ANY)],
-        out_specs=pl.BlockSpec(memory_space=pl.ANY),
-        scratch_shapes=[vmem(velocity.shape, F32), dma((12,)), dma((12,))],
-        compiler_params=pltpu.CompilerParams(vmem_limit_bytes=60 * 1024 * 1024),
-        name="finish",
-    )(result)
-
 
 def solution(mesh):
     return jax.shard_map(

time: 51.7 us -> 48.9 us (0.946)
  Pallas kernels: 51.2 us -> 47.1 us
  local copies, waits for them, and re-layouts: 0 us -> 1.67 us
    pallas_call x2 -> x1, Pallas kernels: 51.2 us -> 47.1 us  [local(): pl.pallas_call(functools.partial(whole_kernel, nx, ny), out_shape=vmem(ve...]
    unnamed x0 -> x1, local copies, waits for them, and re-layouts: none -> 1.67 us
where the time goes in v2:
time: 48.9 us; the launch traced here: 48.8 us
  Pallas kernels  47.1 us (96%)
  local copies, waits for them, and re-layouts  1.67 us (3%)
    pallas_call x1, Pallas kernels, local(): pl.pallas_call(functools.partial(whole_kernel, nx, ny), out_shape=vmem(ve...  47.1 us
    unnamed x1, local copies, waits for them, and re-layouts  1.67 us

profile of v2, /device:TPU:1, one launch (start us, length us, event | category | flops | bytes accessed | tf_op | source)
XLA Modules:
  0.0 48.8 jit_solution(11502999773077691681)
XLA Ops:
  0.0 47.1 %section.1 = f32[3,16,128,128]{3,2,1,0:T(8,128)S(1)} custom-call(f32[3,16,128,128]{3,2,1,0:T(8,128)} %v_hbm.1, f32[128,128]{1,0:T(8,128)} %ix_hbm.1, f32[128,128]{1,0:T(8,128)} %iy_hbm.1, f32[2,128]{1,0:T(2,128)} %bitcast.6, f32[2,128]{1,0:T(2,128)} %bitcast.7, bf16[3,2048]{1,0:T(4,128)(2,1)} %f_hbm.1, bf16[2048,128]{1,0:T(8,128)(2,1)} %k_hbm.1, ...), custom_call_target="tpu_custom_call" | custom-call | tf_op jit(solution)/shard_map/section/pallas_call | solution.py:510
  47.1 1.7 %copy.11 = f32[3,16,128,128]{3,2,1,0:T(8,128)} copy(f32[3,16,128,128]{3,2,1,0:T(8,128)S(1)} %section.1) | data formatting | bytes 6291456

commit v3 on v2

--- a/solution.py
+++ b/solution.py
@@ -12,7 +12,6 @@
 F32, BF16 = jnp.float32, jnp.bfloat16
 N = 128
 CAP = 128
-BLOCK = CAP + 16
 NEAR, FAR = 7.0 / 9.0, 1.0 / 36.0
 
 
@@ -135,7 +134,7 @@
                  edge_ref, low_ref, high_ref, ex_ref, ey_ref, got_x, got_y, reply_x, reply_y,
                  tile_ref, pick_ref, left_x, left_ex, right_y, right_ey, ext_y,
                  send_m, recv_m, send_x, recv_x, send_y, recv_y,
-                 back_send_x, back_recv_x, back_send_y, back_recv_y, edge_send, edge_recv):
+                 back_send_x, back_recv_x, back_send_y, back_recv_y, edge_send, edge_recv, mf_ref, got_mf, send_f, recv_f):
     gx, gy = lax.axis_index("gx"), lax.axis_index("gy")
     depth = v_ref.shape[1]
     half = depth // 2
@@ -174,6 +173,9 @@
 
     def out_m(to, origin):
         return remote(mk_ref.at[to], got_mk.at[origin], send_m.at[to], recv_m.at[origin], (to, gy))
+
+    def out_f(to, origin):
+        return remote(mf_ref.at[to], got_mf.at[origin], send_f.at[to], recv_f.at[origin], (to, gy))
 
     def back_x(to, origin):
         return remote(reply_x.at[to], ex_ref.at[pl.ds(origin * zx, zx)], back_send_x.at[to], back_recv_x.at[origin], (to, gy))
@@ -204,11 +206,9 @@
 
         cell = row_ref[k : k + 1, :]
         plane = cell // N
-        upper = plane >= half
         three = f_ref[:, k * N : (k + 1) * N].astype(F32)
         facts = jnp.concatenate(
-            [jnp.where(upper, 0.0, three), jnp.where(upper, three, 0.0),
-             (plane % half).astype(F32), (cell % N).astype(F32)],
+            [three, plane.astype(F32), (cell % N).astype(F32), jnp.zeros((3, N), F32)],
             axis=0,
         )
         wide_ref[k * N : (k + 1) * N, 0:N] = k_ref[k * N : (k + 1) * N, :]
@@ -247,17 +247,19 @@
                 off = step * per + i
                 to = lax.rem(gx + off, nx)
                 part = rows[i * CAP : (i + 1) * CAP]
-                mk_ref[to, 0:CAP, :] = part[:, :N].astype(BF16)
-                facts_t = part[:, N:].T[0:8, :]
-                mk_ref[to, CAP:, :] = jnp.concatenate([facts_t, jnp.zeros((8, N), F32)], axis=0).astype(BF16)
+                mk_ref[to] = part[:, :N].astype(BF16)
+                facts_t = part[:, N:].T
+                mf_ref[to] = jnp.concatenate([facts_t[0:3], facts_t[3:4] * N + facts_t[4:5]], axis=0)
 
                 @pl.when(off > 0)
                 def _():
                     out_m(to, gx).start()
+                    out_f(to, gx).start()
 
                 @pl.when(off == 0)
                 def _():
                     got_mk[gx] = mk_ref[gx]
+                    got_mf[gx] = mf_ref[gx]
 
     cuts = (0, max(1, rounds // 4), max(1, 3 * rounds // 4), rounds)
     compact(cuts[0], cuts[1])
@@ -334,7 +336,7 @@
     choice = jnp.full((), 0.5, BF16)
 
     def scatter_one(first, many):
-        facts = []
+        facts, cells = [], []
         for i in range(many):
             off = first + i
             source = lax.rem(gx + nx - off, nx)
@@ -342,17 +344,22 @@
             @pl.when(off > 0)
             def _():
                 out_m(gx, source).wait_recv()
-
-            facts.append(got_mk[source, CAP:, :].astype(F32)[0:8])
+                out_f(gx, source).wait_recv()
+
+            got = got_mf[source]
+            upper = got[3:4] >= float(half * N)
+            facts += [jnp.where(upper, 0.0, got[0:3]), jnp.where(upper, got[0:3], 0.0), jnp.zeros((2, N), F32)]
+            cells.append(jnp.where(upper, got[3:4] - float(half * N), got[3:4]))
         stack = jnp.concatenate(facts, axis=0)
         columns = jnp.tile(stack, (N // (8 * many), 1)).T.astype(BF16)
         for i in range(many):
             source = lax.rem(gx + nx - (first + i), nx)
-            rows = got_mk[source, 0:CAP, :]
+            rows = got_mk[source]
             for k in range(6):
                 tile_ref[i * CAP : (i + 1) * CAP, k * N : (k + 1) * N] = rows * columns[:, 8 * i + k : 8 * i + k + 1]
             for zz in range(half):
-                mine = jnp.where(facts[i][6:7] == float(zz), facts[i][7:8], -1.0).astype(BF16)
+                x = cells[i] - float(zz * N)
+                mine = jnp.where((x >= 0.0) & (x < float(N)), x, -1.0).astype(BF16)
                 pick_ref[zz * N : (zz + 1) * N, i * CAP : (i + 1) * CAP] = jnp.where(mine == slot, choice, jnp.zeros((), BF16))
         for h in range(2):
             for r in range(2):
@@ -489,6 +496,7 @@
     @pl.loop(1, nx)
     def _(i):
         out_m(lax.rem(gx + i, nx), gx).wait_send()
+        out_f(lax.rem(gx + i, nx), gx).wait_send()
 
     @pl.when(gx < nx - 1)
     def _():
@@ -516,8 +524,8 @@
             dma((len(args),)),
             vmem((slots, 2 * N), BF16),
             vmem((8, slots), F32),
-            vmem((nx, BLOCK, N), BF16),
-            vmem((nx, BLOCK, N), BF16),
+            vmem((nx, CAP, N), BF16),
+            vmem((nx, CAP, N), BF16),
             vmem((depth, 8, N), F32),
             vmem((depth, 3, 8, N), F32),
             vmem((3 * N, N), F32),
@@ -539,6 +547,7 @@
             vmem((3 * N, 2 * N), BF16),
             dma((nx,)), dma((nx,)), dma((sx,)), dma((nx,)), dma((ny,)), dma((ny,)),
             dma((nx,)), dma((sx,)), dma((ny,)), dma((ny,)), dma((2,)), dma((2,)),
+            vmem((nx, 4, N), F32), vmem((nx, 4, N), F32), dma((nx,)), dma((nx,)),
         ],
         compiler_params=pltpu.CompilerParams(vmem_limit_bytes=56 * 1024 * 1024, collective_id=0, has_side_effects=True),
         name="section",

time: 48.9 us -> 48.8 us (level)
  no operation moved by 1% of the time
where the time goes in v3:
time: 48.8 us; the launch traced here: 48.6 us
  Pallas kernels  46.9 us (96%)
  local copies, waits for them, and re-layouts  1.67 us (3%)
    pallas_call x1, Pallas kernels, local(): pl.pallas_call(functools.partial(whole_kernel, nx, ny), out_shape=vmem(ve...  46.9 us
    unnamed x1, local copies, waits for them, and re-layouts  1.67 us

profile of v3, /device:TPU:1, one launch (start us, length us, event | category | flops | bytes accessed | tf_op | source)
XLA Modules:
  0.0 48.6 jit_solution(6400651251268432524)
XLA Ops:
  0.0 46.9 %section.1 = f32[3,16,128,128]{3,2,1,0:T(8,128)S(1)} custom-call(f32[3,16,128,128]{3,2,1,0:T(8,128)} %v_hbm.1, f32[128,128]{1,0:T(8,128)} %ix_hbm.1, f32[128,128]{1,0:T(8,128)} %iy_hbm.1, f32[2,128]{1,0:T(2,128)} %bitcast.6, f32[2,128]{1,0:T(2,128)} %bitcast.7, bf16[3,2048]{1,0:T(4,128)(2,1)} %f_hbm.1, bf16[2048,128]{1,0:T(8,128)(2,1)} %k_hbm.1, ...), custom_call_target="tpu_custom_call" | custom-call | tf_op jit(solution)/shard_map/section/pallas_call | solution.py:518
  46.9 1.7 %copy.11 = f32[3,16,128,128]{3,2,1,0:T(8,128)} copy(f32[3,16,128,128]{3,2,1,0:T(8,128)S(1)} %section.1) | data formatting | bytes 6291456
